TPU v7x, 32 devices: a whole 2x2x4 slice. The times are simulated.
32 devices in a mesh: child: 2 (over core), row: 4 (over y, x), col: 4 (over z).
Axes of the slice: x: 2, y: 2, z: 4, core: 2. Of those that a mesh axis runs over, the one named last changes fastest.
Arguments:
- child_fronts: float32 [2, 4096, 4096], P('child', 'row', 'col'), as said below
- root_front: float32 [8192, 8192], P('col', ('child', 'row')), as said below
- block_maps: int32 [2, 24], replicated, may hold values from 0 to 63, as said below
Outputs:
- child_factor: float32 [2, 4096, 1024], P('child', 'row')
- root_factor: float32 [8192, 512], P('col')
- root_trailing: float32 [8192, 8192], P('col', ('child', 'row'))
Inputs may be any that keep to these rules, and one draw needn't show every extreme that they name: `block_maps`: row c lists 24 different root blocks in increasing order; block 0 appears in the first row and the last root block in the last row. `child_fronts`: each front is symmetric and positive definite. `root_front`: symmetric and positive definite.
All inputs are finite; a program needn't handle non-finite values.
Results may differ from a plain program's by a relative error of at most 0.0003.
Values may be sent and summed in bfloat16 or wider, within the bound.
A program may use at most 256 MiB of HBM per device.

v0:
```python
import jax
import jax.numpy as jnp
from jax import lax
from jax.sharding import PartitionSpec as P

R = 8192
PANEL = 512
CPAN = 2
BLK = 128
PIV = 1024
NCB = 24


def from_root(block, axis, holder):
    block = jnp.where(lax.axis_index(axis) == holder, block, jnp.zeros_like(block))
    return lax.psum(block, axis)


def lookup(table, first_idx, second_idx):
    hits = (first_idx[..., None, None] == jnp.arange(table.shape[0], dtype=jnp.int32)[:, None]) & (
        second_idx[..., None, None] == jnp.arange(table.shape[1], dtype=jnp.int32)[None, :]
    )
    return jnp.sum(jnp.where(hits, table, 0), axis=(-2, -1))


def panel_step(local_tile, first_col, is_root):
    row_block, col_block = local_tile.shape
    if is_root:
        row_pos = lax.axis_index("col")
        col_pos = lax.axis_index(("child", "row"))
    else:
        row_pos = lax.axis_index("row")
        col_pos = lax.axis_index("col")
    panel_width = min(PANEL, col_block)
    offset = first_col % col_block if col_block >= PANEL else 0
    portion = lax.slice_in_dim(local_tile, offset, offset + panel_width, axis=1)
    arrived = []
    for member in range(max(PANEL // col_block, 1)):
        holder = first_col // col_block + member
        if is_root:
            arrived.append(from_root(portion, ("child", "row"), holder))
        else:
            arrived.append(from_root(portion, "col", holder))
    panel_rows = jnp.concatenate(arrived, axis=1)
    diag_width = min(PANEL, row_block)
    diag_offset = first_col % row_block if row_block >= PANEL else 0
    diag_portion = lax.slice_in_dim(panel_rows, diag_offset, diag_offset + diag_width, axis=0)
    diag_parts = []
    for member in range(max(PANEL // row_block, 1)):
        holder = first_col // row_block + member
        if is_root:
            diag_parts.append(from_root(diag_portion, "col", holder))
        else:
            diag_parts.append(from_root(diag_portion, "row", holder))
    diagonal = jnp.concatenate(diag_parts, axis=0)
    diag_factor = jnp.linalg.cholesky(diagonal)
    solved = lax.linalg.triangular_solve(
        diag_factor, panel_rows, left_side=False, lower=True, transpose_a=True
    )
    row_ids = row_pos * row_block + jnp.arange(row_block, dtype=jnp.int32)
    factor_rows = jnp.where(row_ids[:, None] >= first_col, solved, 0.0)
    update_rows = jnp.where(row_ids[:, None] >= first_col + PANEL, solved, 0.0).astype(jnp.bfloat16)
    if is_root:
        all_rows = lax.all_gather(update_rows, "col", axis=0, tiled=True)
    else:
        all_rows = lax.all_gather(update_rows, "row", axis=0, tiled=True)
    column_rows = lax.dynamic_slice_in_dim(all_rows, col_pos * col_block, col_block, 0)
    update = lax.dot_general(
        update_rows, column_rows, (((1,), (1,)), ((), ())), preferred_element_type=jnp.float32
    )
    return (local_tile - update, factor_rows)


def local(child_fronts, root_front, block_maps):
    local_tile = child_fronts[0]
    factors = []
    for panel_index in range(CPAN):
        local_tile, factor_rows = panel_step(local_tile, panel_index * PANEL, False)
        factors.append(factor_rows)
    child_factor = jnp.concatenate(factors, axis=1)[None]
    row_block, col_block = local_tile.shape
    child_pos = lax.axis_index("child")
    col_pos = lax.axis_index("col")
    row_count = lax.axis_size("row")
    group_count = lax.axis_size(("child", "row"))
    col_count = lax.axis_size("col")
    row_blocks = row_block // BLK
    root_blocks = R // BLK
    target_blocks = R // col_count // BLK
    width_out = R // group_count
    sources = jnp.arange(group_count, dtype=jnp.int32)
    front_blocks = (sources % row_count)[:, None] * row_blocks + jnp.arange(
        row_blocks, dtype=jnp.int32
    )[None, :]
    contrib_rows = front_blocks - PIV // BLK
    source_child = jnp.broadcast_to((sources // row_count)[:, None], contrib_rows.shape)
    row_targets = lookup(block_maps, source_child, contrib_rows)
    row_valid = contrib_rows >= 0
    block_ids = jnp.arange(root_blocks, dtype=jnp.int32)
    full_rows = lax.all_gather(local_tile, "col", axis=1, tiled=True)
    contrib = full_rows[:, PIV:].reshape(row_block, NCB, BLK)
    col_targets = lookup(
        block_maps, jnp.full((NCB,), child_pos, dtype=jnp.int32), jnp.arange(NCB, dtype=jnp.int32)
    )
    col_table = (col_targets[:, None] == block_ids[None, :]).astype(jnp.float32)
    placed = jnp.einsum("ray,am->rmy", contrib, col_table, precision=lax.Precision.HIGHEST).reshape(
        row_block, group_count, width_out
    )
    keep_rows = row_valid & (row_targets // target_blocks == col_pos)
    row_table = (
        keep_rows[:, :, None]
        & (
            (row_targets % target_blocks)[:, :, None]
            == jnp.arange(target_blocks, dtype=jnp.int32)[None, None, :]
        )
    ).astype(jnp.float32)
    received = lax.all_to_all(placed, ("child", "row"), split_axis=1, concat_axis=0, tiled=True)
    count_cols = received.shape[2]
    stacked = received.reshape(group_count, row_blocks, BLK, count_cols)
    summed = jnp.einsum("stq,stxn->qxn", row_table, stacked, precision=lax.Precision.HIGHEST)
    added = summed.reshape(target_blocks * BLK, count_cols)
    assembled = root_front + added
    panel_index = 0
    assembled, factor_rows = panel_step(assembled, panel_index * PANEL, True)
    return (child_factor, factor_rows, assembled)


def solution(mesh):
    return jax.shard_map(
        local,
        mesh=mesh,
        in_specs=(P("child", "row", "col"), P("col", ("child", "row")), P()),
        out_specs=(P("child", "row", None), P("col", None), P("col", ("child", "row"))),
        check_vma=False,
    )
```

profile of v0, /device:TPU:24, one launch (start us, length us, event | category | flops | bytes accessed | tf_op | source)
XLA Modules:
  0.0 2019.6 jit_solution(6126971622012938003)
XLA Ops:
  7.2 5.3 copy.50
  12.6 3.2 slice_select_fusion.2
  15.8 85.6 %all-reduce.8.cloned.1.call-done = f32[1024,512]{0,1:T(8,128)} async-done(((f32[1024,512]{0,1:T(8,128)}), f32[1024,512]{0,1:T(8,128)}) %all-reduce.8.cloned.1.call-update) | async-done | bytes 2097168 | tf_op jit(solution)/shard_map/psum | solution.py:16
  103.9 55.0 %all-reduce.10.cloned.1.call-done = f32[512,512]{0,1:T(8,128)} async-done(((f32[512,512]{0,1:T(8,128)}), f32[512,512]{0,1:T(8,128)}) %all-reduce.10.cloned.1.call-update) | async-done | bytes 1048592 | tf_op jit(solution)/shard_map/psum | solution.py:16
  161.9 11.7 cholesky.374
  173.7 9.8 custom-call.34
  185.4 11.7 cholesky.393
  197.1 10.0 custom-call.35
  208.7 11.7 cholesky.414
  221.1 9.8 custom-call.36
  232.4 11.7 cholesky.431
  249.4 11.4 while.6
  260.8 39.3 %custom-call.37 = f32[4,128,128]{1,2,0:T(8,128)S(1)} custom-call(f32[4,128,128]{2,1,0:T(8,128)S(1)} %get-tuple-element.27), custom_call_target="InvertDiagBlocksLowerTriangular" | custom-call | tf_op jit(solution)/shard_map/triangular_solve/custom-call.3 | solution.py:57
  305.4 2.3 fusion.28
  310.4 52.8 %all-gather.5.cloned.1.call-done = bf16[4096,512]{0,1:T(8,128)(2,1)} async-done(((bf16[1024,512]{0,1:T(8,128)(2,1)}), bf16[4096,512]{0,1:T(8,128)(2,1)}) %all-gather.5.cloned.1.call-update) | async-done | bytes 4194320 | tf_op jit(solution)/shard_map/all_gather | solution.py:66
  363.2 4.2 convolution_subtract_fusion.4
  371.1 84.7 %all-reduce.12.cloned.1.call-done = f32[1024,512]{0,1:T(8,128)} async-done(((f32[1024,512]{0,1:T(8,128)}), f32[1024,512]{0,1:T(8,128)}) %all-reduce.12.cloned.1.call-update) | async-done | bytes 2097168 | tf_op jit(solution)/shard_map/psum | solution.py:16
  458.3 54.4 %all-reduce.14.cloned.1.call-done = f32[512,512]{0,1:T(8,128)} async-done(((f32[512,512]{0,1:T(8,128)}), f32[512,512]{0,1:T(8,128)}) %all-reduce.14.cloned.1.call-update) | async-done | bytes 1048592 | tf_op jit(solution)/shard_map/psum | solution.py:16
  515.7 11.7 cholesky.446
  527.6 9.8 custom-call.38
  538.1 11.7 cholesky.465
  551.2 10.0 custom-call.39
  561.9 11.7 cholesky.486
  574.3 9.8 custom-call.40
  584.7 11.7 cholesky.503
  600.3 8.1 while.7
  610.1 40.1 %custom-call.41 = f32[4,128,128]{1,2,0:T(8,128)S(1)} custom-call(f32[4,128,128]{2,1,0:T(8,128)} %copy-done.22), custom_call_target="InvertDiagBlocksLowerTriangular" | custom-call | tf_op jit(solution)/shard_map/triangular_solve/custom-call.3 | solution.py:57
  656.7 2.3 fusion.25
  661.8 52.8 %all-gather.7.cloned.1.call-done = bf16[4096,512]{0,1:T(8,128)(2,1)} async-done(((bf16[1024,512]{0,1:T(8,128)(2,1)}), bf16[4096,512]{0,1:T(8,128)(2,1)}) %all-gather.7.cloned.1.call-update) | async-done | bytes 4194320 | tf_op jit(solution)/shard_map/all_gather | solution.py:66
  714.6 6.2 convolution_subtract_fusion.3
  721.6 283.0 %all-gather.9.cloned.1.call-done = f32[1024,4096]{0,1:T(8,128)} async-done(((f32[1024,1024]{0,1:T(8,128)}), f32[1024,4096]{0,1:T(8,128)}) %all-gather.9.cloned.1.call-update) | async-done | bytes 16777232 | tf_op jit(solution)/shard_map/all_gather | solution.py:100
  1004.6 11.9 slice.224
  1016.5 12.7 copy.61
  1029.2 22.1 %convolution_bitcast_fusion = f32[1024,64,128]{2,1,0:T(8,128)} fusion(f32[1024,24,128]{2,1,0:T(8,128)} %copy.61, s32[24]{0:T(128)S(1)} %select_reduce_fusion.13), kind=kOutput, calls=%fused_computation.6 | convolution fusion | flops 2415920640 | bytes 46137440 | tf_op jit(solution)/shard_map/ray,am->rmy/dot_general | solution.py:106
  1051.3 35.4 %reshape.207 = f32[1024,8,1024]{2,1,0:T(8,128)} reshape(f32[1024,64,128]{2,1,0:T(8,128)} %convolution_bitcast_fusion) | data formatting | bytes 67108864 | tf_op jit(solution)/shard_map/reshape | solution.py:106
  1086.7 31.7 %copy.62 = f32[1024,8,1024]{2,0,1:T(8,128)} copy(f32[1024,8,1024]{2,1,0:T(8,128)} %reshape.207) | data formatting | bytes 67108864 | tf_op jit(solution)/shard_map/reshape | solution.py:106
  1118.4 7.1 all-to-all-start
  1125.5 9.3 copy.65
  1135.5 353.2 %all-to-all-done = f32[1024,8,1024]{2,0,1:T(8,128)} async-done(((f32[1024,8,1024]{2,0,1:T(8,128)}), f32[1024,8,1024]{2,0,1:T(8,128)}, u32[]{:S(2)}, u32[]{:S(2)}) %all-to-all-start) | async-done | bytes 33554464 | tf_op jit(solution)/shard_map/all_to_all | solution.py:117
  1488.7 32.2 %copy.90 = f32[8,8,128,1024]{2,1,0,3:T(8,128)} copy(f32[8,8,128,1024]{3,2,1,0:T(8,128)} %bitcast.32) | data formatting | bytes 67108864 | tf_op jit(solution)/shard_map/reshape | solution.py:119
  1520.9 19.4 fusion.104
  1540.3 13.9 bitcast_add_fusion
  1554.1 4.7 slice_select_fusion
  1558.9 81.1 %all-reduce.16.cloned.1.call-done = f32[2048,512]{0,1:T(8,128)} async-done(((f32[2048,512]{0,1:T(8,128)}), f32[2048,512]{0,1:T(8,128)}) %all-reduce.16.cloned.1.call-update) | async-done | bytes 4194320 | tf_op jit(solution)/shard_map/psum | solution.py:16
  1642.8 50.7 %all-reduce.18.cloned.1.call-done = f32[512,512]{0,1:T(8,128)} async-done(((f32[512,512]{0,1:T(8,128)}), f32[512,512]{0,1:T(8,128)}) %all-reduce.18.cloned.1.call-update) | async-done | bytes 1048592 | tf_op jit(solution)/shard_map/psum | solution.py:16
  1696.6 11.7 cholesky.518
  1708.3 9.8 custom-call.42
  1718.8 11.7 cholesky.537
  1730.9 10.0 custom-call.43
  1741.9 11.7 cholesky.558
  1753.8 9.8 custom-call.44
  1764.4 11.9 cholesky.575
  1781.8 8.4 while.5
  1790.2 39.3 %custom-call.26 = f32[4,128,128]{1,2,0:T(8,128)S(1)} custom-call(f32[4,128,128]{2,1,0:T(8,128)S(1)} %get-tuple-element.20), custom_call_target="InvertDiagBlocksLowerTriangular" | custom-call | tf_op jit(solution)/shard_map/triangular_solve | solution.py:57
  1829.5 2.3 fusion.33
  1831.9 2.5 convolution_subtract_fusion.2
  1838.7 3.4 fusion.6
  1848.2 2.5 maximum_bitcast_fusion
  1850.7 5.5 copy.79
  1856.2 3.8 fusion.9
  1860.0 5.9 copy.80
  1865.9 127.9 %all-gather.11.cloned.1.call-done = bf16[8192,512]{0,1:T(8,128)(2,1)} async-done(((bf16[2048,512]{0,1:T(8,128)(2,1)}), bf16[8192,512]{0,1:T(8,128)(2,1)}) %all-gather.11.cloned.1.call-update) | async-done | bytes 8388624 | tf_op jit(solution)/shard_map/all_gather | solution.py:64
  1993.7 9.3 convolution_subtract_fusion
  2003.1 9.2 copy.81
  (233 shorter events, 98.2 us)
Async XLA Ops:
  7.2 94.3 %all-reduce.8.cloned.1.call-start = ((), (), s32[]{:S(2)}) async-start(), calls=%async_computation.1 | async-start | bytes 4194304 | tf_op jit(solution)/shard_map/psum | solution.py:16
  15.8 143.1 %all-reduce.10.cloned.1.call-start = ((), (), s32[]{:S(2)}) async-start(), calls=%async_computation.2 | async-start | bytes 2097152 | tf_op jit(solution)/shard_map/psum | solution.py:16
  103.8 259.5 %all-gather.5.cloned.1.call-start = ((), (), s32[]{:S(2)}) async-start(), calls=%async_computation.3 | async-start | bytes 5242880 | tf_op jit(solution)/shard_map/all_gather | solution.py:66
  103.9 204.4 %copy-start.23 = (pred[1024]{0:T(1024)(128)(4,1)}, pred[1024]{0:T(1024)(128)(4,1)S(1)}, u32[]{:S(2)}) copy-start(pred[1024]{0:T(1024)(128)(4,1)S(1)} %fusion.115) | copy-start | bytes 3076
  161.9 21.7 %copy-start.21 = (f32[512,512]{1,0:T(8,128)}, f32[512,512]{1,0:T(8,128)S(1)}, u32[]{:S(2)}) copy-start(f32[512,512]{1,0:T(8,128)S(1)} %fusion.43) | copy-start | bytes 3145732
  184.0 116.2 %copy-start.14 = (f32[1024,512]{0,1:T(8,128)S(1)}, f32[1024,512]{0,1:T(8,128)}, u32[]{:S(2)}) copy-start(f32[1024,512]{0,1:T(8,128)} %all-reduce.8.cloned.1.call-done) | copy-start | bytes 6291460
  300.8 7.5 copy-start.2
  303.0 5.3 copy-start.6
  305.4 3.0 copy-start.10
  308.3 0.8 copy-start.16
  310.4 145.3 %all-reduce.12.cloned.1.call-start = ((), (), s32[]{:S(2)}) async-start(), calls=%async_computation.4 | async-start | bytes 4194304 | tf_op jit(solution)/shard_map/psum | solution.py:16
  367.5 2.0 copy-start
  371.0 141.7 %all-reduce.14.cloned.1.call-start = ((), (), s32[]{:S(2)}) async-start(), calls=%async_computation.5 | async-start | bytes 2097152 | tf_op jit(solution)/shard_map/psum | solution.py:16
  458.0 256.5 %all-gather.7.cloned.1.call-start = ((), (), s32[]{:S(2)}) async-start(), calls=%async_computation.6 | async-start | bytes 5242880 | tf_op jit(solution)/shard_map/all_gather | solution.py:66
  600.3 54.0 %copy-start.15 = (f32[1024,512]{0,1:T(8,128)S(1)}, f32[1024,512]{0,1:T(8,128)}, u32[]{:S(2)}) copy-start(f32[1024,512]{0,1:T(8,128)} %all-reduce.12.cloned.1.call-done) | copy-start | bytes 6291460
  608.5 0.7 copy-start.22
  609.2 1.0 copy-start.20
  654.3 5.4 copy-start.7
  656.7 2.9 copy-start.11
  659.6 0.8 copy-start.17
  661.7 342.9 %all-gather.9.cloned.1.call-start = ((), (), s32[]{:S(2)}) async-start(), calls=%async_computation.7 | async-start | bytes 20971520 | tf_op jit(solution)/shard_map/all_gather | solution.py:100
  720.7 0.7 copy-start.25
  1118.4 370.3 %all-to-all-start = ((f32[1024,8,1024]{2,0,1:T(8,128)}), f32[1024,8,1024]{2,0,1:T(8,128)}, u32[]{:S(2)}, u32[]{:S(2)}) async-start(f32[1024,8,1024]{2,0,1:T(8,128)} %copy.62), calls=%async_computation | async-start | bytes 67108864 | tf_op jit(solution)/shard_map/all_to_all | solution.py:117
  1125.5 514.6 %all-reduce.16.cloned.1.call-start = ((), (), s32[]{:S(2)}) async-start(), calls=%async_computation.8 | async-start | bytes 8388608 | tf_op jit(solution)/shard_map/psum | solution.py:16
  1558.9 134.6 %all-reduce.18.cloned.1.call-start = ((), (), s32[]{:S(2)}) async-start(), calls=%async_computation.9 | async-start | bytes 2097152 | tf_op jit(solution)/shard_map/psum | solution.py:16
  1642.4 351.4 %all-gather.11.cloned.1.call-start = ((), (), s32[]{:S(2)}) async-start(), calls=%async_computation.10 | async-start | bytes 10485760 | tf_op jit(solution)/shard_map/all_gather | solution.py:64
  1790.2 41.6 %copy-start.19 = (f32[512,512]{0,1:T(8,128)}, f32[512,512]{0,1:T(8,128)S(1)}, u32[]{:S(2)}) copy-start(f32[512,512]{0,1:T(8,128)S(1)} %get-tuple-element.283) | copy-start | bytes 3145732
  1831.8 3.6 copy-start.13
  1838.7 4.5 copy-start.4
  1843.2 1.0 copy-start.9
  1844.2 2.0 copy-start.3
  1846.1 1.8 copy-start.24
  1846.1 1.8 copy-start.8
  1846.1 1.8 copy-start.12
  1846.1 1.8 copy-start.18
  1850.7 5.5 copy-start.5
  1860.0 133.7 %copy-start.1 = (bf16[2048,512]{0,1:T(8,128)(2,1)S(1)}, bf16[2048,512]{0,1:T(8,128)(2,1)}, u32[]{:S(2)}) copy-start(bf16[2048,512]{0,1:T(8,128)(2,1)} %select_convert_fusion) | copy-start | bytes 6291460
Sparse Core Ops, SparseCore 0:
  15.9 85.5 all-reduce.7
  105.4 53.4 all-reduce.9
  310.5 52.6 all-gather.4
  371.1 84.5 all-reduce.11
  459.2 53.4 all-reduce.13
  661.8 52.6 all-gather.6
  720.9 283.6 all-gather.8
  1559.0 80.9 all-reduce.15
  1643.1 50.3 all-reduce.17
  1846.2 147.4 all-gather.10
where the time goes:
time: 2040 us; the launch traced here: 2020 us
  waiting for transfers between devices  1280 us (63%)
  other arithmetic  406 us (20%)
  local copies, waits for them, and re-layouts  199 us (10%)
  matrix products  101 us (5%)
  between operations  23.3 us (1%)
    psum x6, waiting for transfers between devices, from_root(): return lax.psum(block, axis)  412 us
    all_to_all x1, waiting for transfers between devices, local(): lax.all_to_all(placed, ('child', 'row'), split_axis=1, concat_axis=0, til...  353 us
    all_gather x1, waiting for transfers between devices, local(): full_rows = lax.all_gather(local_tile, 'col', axis=1, tiled=True)  283 us
    another operation x44, other arithmetic, panel_step(): diag_factor = jnp.linalg.cholesky(diagonal)  237 us
    all_gather x1, waiting for transfers between devices, panel_step(): all_rows = lax.all_gather(update_rows, 'col', axis=0, tiled=True)  128 us
    another operation x7, other arithmetic, panel_step(): lax.linalg.triangular_solve(diag_factor, panel_rows, left_side=False, low...  121 us
    all_gather x2, waiting for transfers between devices, panel_step(): all_rows = lax.all_gather(update_rows, 'row', axis=0, tiled=True)  106 us
    reshape x2, local copies, waits for them, and re-layouts, local(): jnp.einsum('ray,am->rmy', contrib, col_table, precision=lax.Precision.HIG...  67.1 us
  transfers between devices with their start and end apart: 11, of which 11 were waited for; matrix products, arithmetic and copies ran while one was open for 1% of the time, Pallas kernels for 0%

commit v1 on v0

v1 whole, which is shorter than its diff:
```python
import functools

import jax
import jax.numpy as jnp
from jax import lax
from jax.experimental import pallas as pl
from jax.experimental.pallas import tpu as pltpu
from jax.sharding import PartitionSpec as P

R = 8192
PANEL = 512
BLK = 128
PIV = 1024
NCB = 24
PB = PIV // BLK
HI = lax.Precision.HIGHEST
VMEM_LIMIT = 48 * 1024 * 1024


def small_inverse(block):
    eye = (
        lax.broadcasted_iota(jnp.int32, (BLK, BLK), 0)
        == lax.broadcasted_iota(jnp.int32, (BLK, BLK), 1)
    ).astype(jnp.float32)
    sub = lax.broadcasted_iota(jnp.int32, (8, BLK), 0)
    left = [block[8 * g : 8 * g + 8, :] for g in range(BLK // 8)]
    right = [eye[8 * g : 8 * g + 8, :] for g in range(BLK // 8)]
    for j in range(BLK):
        first, place = j // 8, j % 8
        row_left = left[first][place : place + 1, :]
        row_right = right[first][place : place + 1, :]
        scale = 1.0 / row_left[:, j : j + 1]
        row_left = row_left * scale
        row_right = row_right * scale
        for g in range(first, BLK // 8):
            column = left[g][:, j : j + 1]
            if g == first:
                if place == 7:
                    continue
                column = jnp.where(sub > place, column, 0.0)
            left[g] = left[g] - column * row_left
            right[g] = right[g] - column * row_right
    pivots = jnp.sum(jnp.concatenate(left, axis=0) * eye, axis=1, keepdims=True)
    return jnp.concatenate(right, axis=0) / jnp.sqrt(pivots)


def chol_kernel(a_ref, inv_ref, work):
    n = PANEL
    work[:, :n] = a_ref[...]
    work[:, n:] = (
        lax.broadcasted_iota(jnp.int32, (n, n), 0) == lax.broadcasted_iota(jnp.int32, (n, n), 1)
    ).astype(jnp.float32)
    ids = lax.broadcasted_iota(jnp.int32, (n, 1), 0)

    def step(k, carry):
        at = pl.multiple_of(k * BLK, BLK)
        here = pl.ds(at, BLK)
        small = small_inverse(work[here, here])
        rows = jnp.dot(small, work[here, :], precision=HI, preferred_element_type=jnp.float32)
        column = lax.dot_general(
            work[:, here], small, (((1,), (1,)), ((), ())), precision=HI,
            preferred_element_type=jnp.float32,
        )
        column = jnp.where(ids >= at + BLK, column, 0.0)
        work[...] = work[...] - jnp.dot(
            column, rows, precision=HI, preferred_element_type=jnp.float32
        )
        inv_ref[here, :] = rows[:, n:]
        return carry

    lax.fori_loop(0, n // BLK, step, 0)


def inverse_factor(diagonal):
    return pl.pallas_call(
        chol_kernel,
        out_shape=jax.ShapeDtypeStruct((PANEL, PANEL), jnp.float32),
        in_specs=[pl.BlockSpec(memory_space=pltpu.VMEM)],
        out_specs=pl.BlockSpec(memory_space=pltpu.VMEM),
        scratch_shapes=[pltpu.VMEM((PANEL, 2 * PANEL), jnp.float32)],
        compiler_params=pltpu.CompilerParams(vmem_limit_bytes=VMEM_LIMIT),
        cost_estimate=pl.CostEstimate(flops=60_000_000_000, bytes_accessed=2 << 20, transcendentals=0),
    )(diagonal)


def place_kernel(src_ref, full_ref, out_ref):
    m = pl.program_id(0) * pl.num_programs(1) + pl.program_id(1)

    @pl.when(src_ref[m] >= 0)
    def _():
        out_ref[...] = full_ref[...]

    @pl.when(src_ref[m] < 0)
    def _():
        out_ref[...] = jnp.zeros_like(out_ref)


def place(source, full, groups, width):
    _, rows, cols = full.shape
    per, inner = width // BLK, cols // BLK

    def pick(g, m, src):
        b = jnp.maximum(src[g * per + m], 0) + PB
        return (b // inner, 0, b % inner)

    return pl.pallas_call(
        place_kernel,
        grid_spec=pltpu.PrefetchScalarGridSpec(
            num_scalar_prefetch=1,
            grid=(groups, per),
            in_specs=[pl.BlockSpec((1, rows, BLK), pick)],
            out_specs=pl.BlockSpec((1, rows, BLK), lambda g, m, src: (g, 0, m)),
        ),
        out_shape=jax.ShapeDtypeStruct((groups, rows, width), full.dtype),
        compiler_params=pltpu.CompilerParams(vmem_limit_bytes=VMEM_LIMIT),
        cost_estimate=pl.CostEstimate(flops=0, bytes_accessed=48 << 20, transcendentals=0),
    )(source, full)


def column_kernel(src_ref, upd_ref, out_ref):
    c, m = pl.program_id(0), pl.program_id(1)

    @pl.when(src_ref[c, m] >= 0)
    def _():
        out_ref[...] = upd_ref[...]

    @pl.when(src_ref[c, m] < 0)
    def _():
        out_ref[...] = jnp.zeros_like(out_ref)


def column_rows(source, updates, row_count):
    _, rows, depth = updates.shape
    per = rows // BLK
    count = source.shape[1]

    def pick(c, m, src):
        a = jnp.maximum(src[c, m], 0) + PB
        return (c * row_count + a // per, a % per, 0)

    return pl.pallas_call(
        column_kernel,
        grid_spec=pltpu.PrefetchScalarGridSpec(
            num_scalar_prefetch=1,
            grid=(2, count),
            in_specs=[pl.BlockSpec((1, BLK, depth), pick)],
            out_specs=pl.BlockSpec((1, BLK, depth), lambda c, m, src: (c, m, 0)),
        ),
        out_shape=jax.ShapeDtypeStruct((2, count * BLK, depth), updates.dtype),
        compiler_params=pltpu.CompilerParams(vmem_limit_bytes=VMEM_LIMIT),
    )(source, updates)


def assemble_kernel(src_ref, root_ref, got0, got1, upd0, upd1, cols_ref, out_ref):
    q = pl.program_id(0)
    out_ref[...] = root_ref[...]
    for c, got, upd in ((0, got0, upd0), (1, got1, upd1)):
        @pl.when(src_ref[c, q] >= 0)
        def _(c=c, got=got, upd=upd):
            update = lax.dot_general(
                upd[0], cols_ref[c], (((1,), (1,)), ((), ())), preferred_element_type=jnp.float32
            )
            out_ref[...] += got[0].astype(jnp.float32) - update


def assemble(source, root, received, updates, columns, row_count):
    height, width = root.shape
    per = received.shape[1] // BLK
    depth = updates.shape[2]

    def pick(c):
        def index(q, src):
            a = jnp.maximum(src[c, q], 0) + PB
            return (c * row_count + a // per, a % per, 0)
        return index

    return pl.pallas_call(
        assemble_kernel,
        grid_spec=pltpu.PrefetchScalarGridSpec(
            num_scalar_prefetch=1,
            grid=(height // BLK,),
            in_specs=[
                pl.BlockSpec((BLK, width), lambda q, src: (q, 0)),
                pl.BlockSpec((1, BLK, width), pick(0)),
                pl.BlockSpec((1, BLK, width), pick(1)),
                pl.BlockSpec((1, BLK, depth), pick(0)),
                pl.BlockSpec((1, BLK, depth), pick(1)),
                pl.BlockSpec((2, width, depth), lambda q, src: (0, 0, 0)),
            ],
            out_specs=pl.BlockSpec((BLK, width), lambda q, src: (q, 0)),
        ),
        out_shape=jax.ShapeDtypeStruct((height, width), jnp.float32),
        compiler_params=pltpu.CompilerParams(vmem_limit_bytes=VMEM_LIMIT),
    )(source, root, received, received, updates, updates, columns)


def dot_t(left, right, precision=None):
    return lax.dot_general(
        left, right, (((1,), (1,)), ((), ())), precision=precision,
        preferred_element_type=jnp.float32,
    )


def local(child_fronts, root_front, block_maps):
    tile = child_fronts[0]
    row_block, col_block = tile.shape
    row_pos, col_pos = lax.axis_index("row"), lax.axis_index("col")
    child_pos = lax.axis_index("child")
    group_pos = lax.axis_index(("child", "row"))
    row_count = lax.axis_size("row")
    groups = lax.axis_size(("child", "row"))
    height, width = root_front.shape
    assert col_block == PIV

    hits = block_maps[:, :, None] == jnp.arange(R // BLK, dtype=jnp.int32)
    inverse = jnp.max(
        jnp.where(hits, jnp.arange(NCB, dtype=jnp.int32)[None, :, None], -1), axis=1
    )
    mine = lax.dynamic_slice_in_dim(inverse, child_pos, 1, 0)[0]
    row_source = lax.dynamic_slice_in_dim(inverse, col_pos * (height // BLK), height // BLK, 1)
    col_source = lax.dynamic_slice_in_dim(inverse, group_pos * (width // BLK), width // BLK, 1)

    if row_block >= PIV:
        corner = jnp.where(row_pos == 0, tile[:PIV], 0.0)
    else:
        corner = jnp.concatenate(
            [jnp.where(row_pos == m, tile, 0.0) for m in range(PIV // row_block)], axis=0
        )
    corner = jnp.where(col_pos == 0, corner, 0.0)
    corner = jnp.concatenate(
        [corner[:PANEL, :PANEL], corner[PANEL:, :PANEL], corner[PANEL:, PANEL:]], axis=0
    )
    corner = lax.psum(corner, ("row", "col"))
    full = lax.all_gather(tile, "col", axis=0)

    inv0 = inverse_factor(corner[:PANEL])
    low = dot_t(corner[PANEL : 2 * PANEL], inv0, HI).astype(jnp.bfloat16)
    inv1 = inverse_factor(corner[2 * PANEL :] - dot_t(low, low))

    placed = place(mine, full, groups, width)
    received = lax.all_to_all(placed, ("child", "row"), split_axis=0, concat_axis=0, tiled=True)

    panel = full[0]
    row_ids = (row_pos * row_block + jnp.arange(row_block, dtype=jnp.int32))[:, None]
    fac0 = dot_t(panel[:, :PANEL], inv0, HI)
    upd0 = jnp.where(row_ids >= PANEL, fac0, 0.0).astype(jnp.bfloat16)
    fac1 = dot_t(panel[:, PANEL:] - dot_t(upd0, low), inv1, HI)
    fac1 = jnp.where(row_ids >= PANEL, fac1, 0.0)
    upd1 = jnp.where(row_ids >= PIV, fac1, 0.0).astype(jnp.bfloat16)
    child_factor = jnp.concatenate([fac0, fac1], axis=1)[None]
    updates = lax.all_gather(jnp.concatenate([upd0, upd1], axis=1), ("child", "row"), axis=0)

    columns = column_rows(col_source, updates, row_count)
    assembled = assemble(row_source, root_front, received, updates, columns, row_count)

    if width >= PANEL:
        own = jnp.where(group_pos == 0, assembled[:, :PANEL], 0.0)
    else:
        own = jnp.concatenate(
            [jnp.where(group_pos == m, assembled, 0.0) for m in range(PANEL // width)], axis=1
        )
    diagonal = lax.psum(jnp.where(col_pos == 0, own[:PANEL], 0.0), ("child", "row", "col"))
    strip = lax.psum(jnp.where(col_pos == 0, assembled[:PANEL], 0.0), "col")
    panel_rows = lax.psum(own, ("child", "row"))
    inv = inverse_factor(diagonal)
    root_factor = dot_t(panel_rows, inv, HI)
    root_ids = (col_pos * height + jnp.arange(height, dtype=jnp.int32))[:, None]
    row_update = jnp.where(root_ids >= PANEL, root_factor, 0.0).astype(jnp.bfloat16)
    col_ids = (group_pos * width + jnp.arange(width, dtype=jnp.int32))[None, :]
    col_update = jnp.dot(inv, strip, precision=HI, preferred_element_type=jnp.float32)
    col_update = jnp.where(col_ids >= PANEL, col_update, 0.0).astype(jnp.bfloat16)
    trailing = assembled - jnp.dot(row_update, col_update, preferred_element_type=jnp.float32)
    return (child_factor, root_factor, trailing)


def solution(mesh):
    return jax.shard_map(
        local,
        mesh=mesh,
        in_specs=(P("child", "row", "col"), P("col", ("child", "row")), P()),
        out_specs=(P("child", "row", None), P("col", None), P("col", ("child", "row"))),
        check_vma=False,
    )
```

time: 2040 us -> 1360 us (0.67)
  other arithmetic: 406 us -> 20.6 us
  waiting for transfers between devices: 1280 us -> 989 us
  Pallas kernels: 0 us -> 233 us
  local copies, waits for them, and re-layouts: 199 us -> 37.4 us
  matrix products: 101 us -> 33.8 us
    all_gather x4 -> x2, waiting for transfers between devices: 516 us -> 77.8 us  [the longest x1 77.8 us: local(): lax.all_gather(jnp.concatenate([upd0, upd1], axis=1), ('child', 'row'), a...]
    another operation x51 -> x0, other arithmetic: 358 us -> none  [the longest x44 237 us: panel_step(): diag_factor = jnp.linalg.cholesky(diagonal)]
    pallas_call x0 -> x6, Pallas kernels: none -> 233 us  [the longest x3 163 us: inverse_factor(): pl.pallas_call(chol_kernel, out_shape=jax.ShapeDtypeStruct((PANEL, PANEL)...]
    psum x6 -> x4, waiting for transfers between devices: 412 us -> 620 us  [the longest x1 407 us: local(): corner = lax.psum(corner, ('row', 'col'))]
    reshape x4 -> x0, local copies, waits for them, and re-layouts: 112 us -> none  [the longest x2 67.1 us: local(): jnp.einsum('ray,am->rmy', contrib, col_table, precision=lax.Precision.HIG...]
    all_to_all x1, waiting for transfers between devices: 353 us -> 290 us  [local(): lax.all_to_all(placed, ('child', 'row'), split_axis=0, concat_axis=0, til...]
    another operation x39 -> x0, matrix products: 39.8 us -> none  [the longest x21 30.9 us: panel_step(): lax.linalg.triangular_solve(diag_factor, panel_rows, left_side=False, low...]
    unnamed x57 -> x13, local copies, waits for them, and re-layouts: 42.3 us -> 10.8 us
  transfers between devices with their start and end apart: 11 -> 7, of which waited for: 11 -> 6; matrix products, arithmetic and copies ran while one was open for 1% -> 4% of each run, Pallas kernels for 0% -> 16%
where the time goes in v1:
time: 1360 us; the launch traced here: 1350 us
  waiting for transfers between devices  989 us (73%)
  Pallas kernels  233 us (17%)
  local copies, waits for them, and re-layouts  37.4 us (3%)
  matrix products  33.8 us (2%)
  other arithmetic  20.6 us (2%)
  between operations  16.2 us (1%)
  starting transfers between devices  15.7 us (1%)
    psum x1, waiting for transfers between devices, local(): corner = lax.psum(corner, ('row', 'col'))  407 us
    all_to_all x1, waiting for transfers between devices, local(): lax.all_to_all(placed, ('child', 'row'), split_axis=0, concat_axis=0, til...  290 us
    pallas_call x3, Pallas kernels, inverse_factor(): pl.pallas_call(chol_kernel, out_shape=jax.ShapeDtypeStruct((PANEL, PANEL)...  163 us
    psum x1, waiting for transfers between devices, local(): lax.psum(jnp.where(col_pos == 0, own[:PANEL], 0.0), ('child', 'row', 'col'))  107 us
    all_gather x1, waiting for transfers between devices, local(): lax.all_gather(jnp.concatenate([upd0, upd1], axis=1), ('child', 'row'), a...  77.8 us
    psum x1, waiting for transfers between devices, local(): strip = lax.psum(jnp.where(col_pos == 0, assembled[:PANEL], 0.0), 'col')  76.8 us
    pallas_call x1, Pallas kernels, place(): pl.pallas_call(place_kernel, grid_spec=pltpu.PrefetchScalarGridSpec(num_s...  41.7 us
    psum x1, waiting for transfers between devices, local(): panel_rows = lax.psum(own, ('child', 'row'))  28.5 us
  transfers between devices with their start and end apart: 7, of which 6 were waited for; matrix products, arithmetic and copies ran while one was open for 4% of the time, Pallas kernels for 16%

profile of v1, /device:TPU:24, one launch (start us, length us, event | category | flops | bytes accessed | tf_op | source)
XLA Modules:
  0.0 1345.6 jit_solution(15002006281910435574)
XLA Ops:
  8.0 0.0 all-reduce.5.cloned.1.call-start
  8.1 2.7 select_bitcast_fusion
  10.8 0.1 slice.47
  10.9 0.2 slice.46
  11.1 2.0 pad_maximum_fusion
  13.1 0.0 copy-start.5
  13.1 0.0 all-reduce.5.cloned.1.call-update
  13.1 0.0 all-gather.4.cloned.1.call-start
  13.2 0.5 all-gather.4.cloned.1.call-update
  13.7 0.0 all-gather.6.cloned.1.call-start
  13.8 0.0 copy-done.5
  13.8 0.1 select_reduce_fusion
  13.9 407.3 %all-reduce.5.cloned.1.call-done = f32[1536,512]{1,0:T(8,128)} async-done(((f32[1536,512]{1,0:T(8,128)}), f32[1536,512]{1,0:T(8,128)}) %all-reduce.5.cloned.1.call-update) | async-done | bytes 3145744 | tf_op jit(solution)/shard_map/psum | solution.py:233
  421.2 1.3 slice.48.a_ref
  422.5 0.0 copy-start.4
  422.5 54.1 %shard_map.58 = f32[512,512]{1,0:T(8,128)S(1)} custom-call(f32[512,512]{1,0:T(8,128)S(1)} %slice.48.a_ref), custom_call_target="tpu_custom_call" | custom-call | flops 60000002048 | bytes 2097152 | tf_op jit(solution)/shard_map/pallas_call | solution.py:75
  476.6 0.0 copy-done.4
  476.6 1.9 convolution_convert_fusion
  478.5 0.5 convolution_subtract_fusion.1.a_ref
  479.0 54.4 %shard_map.59 = f32[512,512]{1,0:T(8,128)S(1)} custom-call(f32[512,512]{1,0:T(8,128)S(1)} %convolution_subtract_fusion.1.a_ref), custom_call_target="tpu_custom_call" | custom-call | flops 60000002048 | bytes 2097152 | tf_op jit(solution)/shard_map/pallas_call | solution.py:75
  533.3 0.0 all-gather.4.cloned.1.call-done.full_ref
  533.4 2.5 slice_bitcast_fusion
  535.9 4.9 select_convert_fusion.4
  540.8 0.8 fusion.14
  541.5 3.6 select_convert_fusion.3
  545.1 1.5 pad_maximum_fusion.1
  546.6 0.0 all-gather.6.cloned.1.call-update
  546.6 41.7 %shard_map.60 = f32[8,1024,1024]{2,1,0:T(8,128)} custom-call(s32[64]{0:T(128)S(1)} %fusion.12.src_ref, f32[4,1024,1024]{2,1,0:T(8,128)} %all-gather.4.cloned.1.call-done.full_ref), custom_call_target="tpu_custom_call" | custom-call | bytes 50331648 | tf_op jit(solution)/shard_map/pallas_call | solution.py:106
  588.4 7.4 all-to-all-start
  595.8 0.0 all-reduce.9.cloned.1.call-start
  595.8 0.1 constant_dynamic-slice_fusion.2.src_ref
  595.9 0.1 constant_dynamic-slice_fusion.src_ref
  596.0 77.8 %all-gather.6.cloned.1.call-done = bf16[8192,1024]{0,1:T(8,128)(2,1)} async-done(((bf16[1024,1024]{0,1:T(8,128)(2,1)}), bf16[8192,1024]{0,1:T(8,128)(2,1)}) %all-gather.6.cloned.1.call-update) | async-done | bytes 16777232 | tf_op jit(solution)/shard_map/all_gather | solution.py:251
  673.8 22.4 %copy.10 = bf16[8192,1024]{1,0:T(8,128)(2,1)} copy(bf16[8192,1024]{0,1:T(8,128)(2,1)} %all-gather.6.cloned.1.call-done) | data formatting | bytes 33554432 | tf_op jit(solution)/shard_map/all_gather | solution.py:251
  696.1 7.1 shard_map.61.cols_ref
  703.2 0.0 copy-start
  703.2 2.0 copy-done
  705.2 290.1 %all-to-all-done.got0.got1 = f32[8,1024,1024]{2,1,0:T(8,128)} async-done(((f32[8,1024,1024]{2,1,0:T(8,128)}), f32[8,1024,1024]{2,1,0:T(8,128)}, u32[]{:S(2)}, u32[]{:S(2)}) %all-to-all-start) | async-done | bytes 33554464 | tf_op jit(solution)/shard_map/all_to_all | solution.py:241
  995.4 0.0 copy-start.1
  995.4 2.2 copy-done.1
  997.6 21.5 %shard_map.62 = f32[2048,1024]{1,0:T(8,128)} custom-call(s32[2,16]{1,0:T(2,128)S(1)} %constant_dynamic-slice_fusion.2.src_ref, f32[2048,1024]{1,0:T(8,128)} %root_ref.1, f32[8,1024,1024]{2,1,0:T(8,128)} %all-to-all-done.got0.got1, f32[8,1024,1024]{2,1,0:T(8,128)} %all-to-all-done.got0.got1, bf16[8,1024,1024]{2,1,0:T(8,128)(2,1)} %bitcast.24, ...), custom_call_target="tpu_custom_call" | custom-call | tf_op jit(solution)/shard_map/pallas_call | solution.py:177
  1019.1 4.6 slice_select_fusion
  1023.7 2.3 slice_select_fusion.2
  1026.0 0.0 all-reduce.9.cloned.1.call-update
  1026.0 0.0 all-reduce.7.cloned.1.call-start
  1026.1 0.5 all-reduce.7.cloned.1.call-update
  1026.6 8.1 all-reduce.11.cloned.1.call-start
  1034.7 4.1 maximum_bitcast_fusion
  1038.9 5.4 copy.11
  1044.2 3.2 slice_select_fusion.1
  1047.5 0.0 all-reduce.11.cloned.1.call-update
  1047.5 107.4 %all-reduce.9.cloned.1.call-done.a_ref = f32[512,512]{1,0:T(8,128)} async-done(((f32[512,512]{1,0:T(8,128)}), f32[512,512]{1,0:T(8,128)}) %all-reduce.9.cloned.1.call-update) | async-done | bytes 1048592 | tf_op jit(solution)/shard_map/psum | solution.py:262
  1154.8 0.0 copy-start.2
  1154.8 1.2 copy-done.2
  1156.1 54.1 %shard_map.63 = f32[512,512]{1,0:T(8,128)S(1)} custom-call(f32[512,512]{1,0:T(8,128)S(1)} %copy-done.2), custom_call_target="tpu_custom_call" | custom-call | flops 60000002048 | bytes 2097152 | tf_op jit(solution)/shard_map/pallas_call | solution.py:75
  1210.2 28.5 %all-reduce.7.cloned.1.call-done = f32[2048,512]{1,0:T(8,128)} async-done(((f32[2048,512]{1,0:T(8,128)}), f32[2048,512]{1,0:T(8,128)}) %all-reduce.7.cloned.1.call-update) | async-done | bytes 4194320 | tf_op jit(solution)/shard_map/psum | solution.py:264
  1238.7 10.0 fusion.15
  1248.8 76.8 %all-reduce.11.cloned.1.call-done = f32[512,1024]{1,0:T(8,128)} async-done(((f32[512,1024]{1,0:T(8,128)}), f32[512,1024]{1,0:T(8,128)}) %all-reduce.11.cloned.1.call-update) | async-done | bytes 2097168 | tf_op jit(solution)/shard_map/psum | solution.py:263
  1325.6 0.0 copy-start.3
  1325.6 5.3 select_convert_fusion.2
  1330.9 0.0 copy-done.3
  1330.9 6.9 convolution_subtract_fusion
  (4 shorter events, 0.0 us)
Async XLA Ops:
  8.0 413.2 %all-reduce.5.cloned.1.call-start = ((), (), s32[]{:S(2)}) async-start(), calls=%async_computation.1 | async-start | bytes 6291456 | tf_op jit(solution)/shard_map/psum | solution.py:233
  13.1 0.7 copy-start.5
  13.1 520.3 %all-gather.4.cloned.1.call-start = ((), (), s32[]{:S(2)}) async-start(), calls=%async_computation.2 | async-start | bytes 20971520 | tf_op jit(solution)/shard_map/all_gather | solution.py:234
  13.7 660.1 %all-gather.6.cloned.1.call-start = ((), (), s32[]{:S(2)}) async-start(), calls=%async_computation.6 | async-start | bytes 18874368 | tf_op jit(solution)/shard_map/all_gather | solution.py:251
  422.5 54.1 %copy-start.4 = (f32[1536,512]{1,0:T(8,128)S(1)}, f32[1536,512]{1,0:T(8,128)}, u32[]{:S(2)}) copy-start(f32[1536,512]{1,0:T(8,128)} %all-reduce.5.cloned.1.call-done) | copy-start | bytes 9437188
  588.4 407.0 %all-to-all-start = ((f32[8,1024,1024]{2,1,0:T(8,128)}), f32[8,1024,1024]{2,1,0:T(8,128)}, u32[]{:S(2)}, u32[]{:S(2)}) async-start(f32[8,1024,1024]{2,1,0:T(8,128)} %shard_map.60), calls=%async_computation | async-start | bytes 67108864 | tf_op jit(solution)/shard_map/all_to_all | solution.py:241
  595.8 559.1 %all-reduce.9.cloned.1.call-start = ((), (), s32[]{:S(2)}) async-start(), calls=%async_computation.4 | async-start | bytes 2097152 | tf_op jit(solution)/shard_map/psum | solution.py:262
  703.2 2.0 copy-start
  995.4 2.2 copy-start.1
  1026.0 212.7 %all-reduce.7.cloned.1.call-start = ((), (), s32[]{:S(2)}) async-start(), calls=%async_computation.3 | async-start | bytes 8388608 | tf_op jit(solution)/shard_map/psum | solution.py:264
  1026.6 298.9 %all-reduce.11.cloned.1.call-start = ((), (), s32[]{:S(2)}) async-start(), calls=%async_computation.5 | async-start | bytes 4194304 | tf_op jit(solution)/shard_map/psum | solution.py:263
  1154.8 1.2 copy-start.2
  1325.6 5.3 copy-start.3
Sparse Core Ops, SparseCore 0:
  15.0 406.1 all-reduce.4
  546.7 126.9 all-gather.5
Sparse Core Ops, SparseCore 1:
  15.2 302.7 all-gather.3
  1026.1 128.7 all-reduce.8
  1158.0 80.7 all-reduce.6
  1241.2 84.3 all-reduce.10

commit v2 on v1

--- a/solution.py
+++ b/solution.py
@@ -79,7 +79,7 @@
         out_specs=pl.BlockSpec(memory_space=pltpu.VMEM),
         scratch_shapes=[pltpu.VMEM((PANEL, 2 * PANEL), jnp.float32)],
         compiler_params=pltpu.CompilerParams(vmem_limit_bytes=VMEM_LIMIT),
-        cost_estimate=pl.CostEstimate(flops=60_000_000_000, bytes_accessed=2 << 20, transcendentals=0),
+        cost_estimate=pl.CostEstimate(flops=1_000_000, bytes_accessed=2 << 20, transcendentals=0),
     )(diagonal)
 
 
@@ -160,7 +160,7 @@
             update = lax.dot_general(
                 upd[0], cols_ref[c], (((1,), (1,)), ((), ())), preferred_element_type=jnp.float32
             )
-            out_ref[...] += got[0].astype(jnp.float32) - update
+            out_ref[...] += got[0] - update
 
 
 def assemble(source, root, received, updates, columns, row_count):
@@ -201,6 +201,17 @@
     )
 
 
+def spread(block, col_pos, parts=4):
+    count = lax.axis_size("col")
+    pieces = []
+    for piece in jnp.split(block, parts, axis=0):
+        for hop in range(count - 1):
+            arrived = lax.ppermute(piece, "col", [(hop, hop + 1)])
+            piece = jnp.where(col_pos == hop + 1, arrived, piece)
+        pieces.append(piece)
+    return jnp.concatenate(pieces, axis=0)
+
+
 def local(child_fronts, root_front, block_maps):
     tile = child_fronts[0]
     row_block, col_block = tile.shape
@@ -233,12 +244,17 @@
     corner = lax.psum(corner, ("row", "col"))
     full = lax.all_gather(tile, "col", axis=0)
 
+    largest = lax.pmax(jnp.max(jnp.abs(tile)), ("child", "row", "col"))
+    unscale = jnp.maximum(largest, 1e-30).reshape(1) * (1.0 / 32768.0)
+    placed = (place(mine, full, groups, width) * (1.0 / unscale)).astype(jnp.float16)
+    corner, placed = lax.optimization_barrier((corner, placed))
+
     inv0 = inverse_factor(corner[:PANEL])
     low = dot_t(corner[PANEL : 2 * PANEL], inv0, HI).astype(jnp.bfloat16)
     inv1 = inverse_factor(corner[2 * PANEL :] - dot_t(low, low))
 
-    placed = place(mine, full, groups, width)
     received = lax.all_to_all(placed, ("child", "row"), split_axis=0, concat_axis=0, tiled=True)
+    received = received.astype(jnp.float32) * unscale
 
     panel = full[0]
     row_ids = (row_pos * row_block + jnp.arange(row_block, dtype=jnp.int32))[:, None]
@@ -260,7 +276,7 @@
             [jnp.where(group_pos == m, assembled, 0.0) for m in range(PANEL // width)], axis=1
         )
     diagonal = lax.psum(jnp.where(col_pos == 0, own[:PANEL], 0.0), ("child", "row", "col"))
-    strip = lax.psum(jnp.where(col_pos == 0, assembled[:PANEL], 0.0), "col")
+    strip = spread(assembled[:PANEL], col_pos)
     panel_rows = lax.psum(own, ("child", "row"))
     inv = inverse_factor(diagonal)
     root_factor = dot_t(panel_rows, inv, HI)

time: 1360 us -> 1190 us (0.88)
  waiting for transfers between devices: 989 us -> 719 us
  blocking collectives: 0 us -> 51.5 us
  other arithmetic: 20.6 us -> 62.7 us
    psum x1, waiting for transfers between devices: 407 us -> 42.7 us  [local(): corner = lax.psum(corner, ('row', 'col'))]
    all_gather x1, waiting for transfers between devices: 0.03 us -> 253 us  [local(): full = lax.all_gather(tile, 'col', axis=0)]
    all_gather x1, waiting for transfers between devices: 77.8 us -> 0.01 us  [local(): lax.all_gather(jnp.concatenate([upd0, upd1], axis=1), ('child', 'row'), a...]
    psum x1 -> x0, waiting for transfers between devices: 76.8 us -> none  [local(): strip = lax.psum(jnp.where(col_pos == 0, assembled[:PANEL], 0.0), 'col')]
    pmax x0 -> x1, blocking collectives: none -> 51.5 us  [local(): largest = lax.pmax(jnp.max(jnp.abs(tile)), ('child', 'row', 'col'))]
    ppermute x0 -> x12, waiting for transfers between devices: none -> 41.4 us  [spread(): arrived = lax.ppermute(piece, 'col', [(hop, hop + 1)])]
    all_to_all x1, waiting for transfers between devices: 290 us -> 251 us  [local(): lax.all_to_all(placed, ('child', 'row'), split_axis=0, concat_axis=0, til...]
    psum x1, waiting for transfers between devices: 28.5 us -> 0.02 us  [local(): panel_rows = lax.psum(own, ('child', 'row'))]
  transfers between devices with their start and end apart: 7 -> 18, of which waited for: 6 -> 8; matrix products, arithmetic and copies ran while one was open for 4% -> 6% of each run, Pallas kernels for 16% -> 8%
where the time goes in v2:
time: 1190 us; the launch traced here: 1170 us
  waiting for transfers between devices  719 us (60%)
  Pallas kernels  232 us (19%)
  other arithmetic  62.7 us (5%)
  blocking collectives  51.5 us (4%)
  local copies, waits for them, and re-layouts  35.3 us (3%)
  matrix products  32.1 us (3%)
  starting transfers between devices  20 us (2%)
  between operations  16.5 us (1%)
    all_gather x1, waiting for transfers between devices, local(): full = lax.all_gather(tile, 'col', axis=0)  253 us
    all_to_all x1, waiting for transfers between devices, local(): lax.all_to_all(placed, ('child', 'row'), split_axis=0, concat_axis=0, til...  251 us
    pallas_call x3, Pallas kernels, inverse_factor(): pl.pallas_call(chol_kernel, out_shape=jax.ShapeDtypeStruct((PANEL, PANEL)...  163 us
    psum x1, waiting for transfers between devices, local(): lax.psum(jnp.where(col_pos == 0, own[:PANEL], 0.0), ('child', 'row', 'col'))  131 us
    pmax x1, blocking collectives, local(): largest = lax.pmax(jnp.max(jnp.abs(tile)), ('child', 'row', 'col'))  51.5 us
    psum x1, waiting for transfers between devices, local(): corner = lax.psum(corner, ('row', 'col'))  42.7 us
    ppermute x12, waiting for transfers between devices, spread(): arrived = lax.ppermute(piece, 'col', [(hop, hop + 1)])  41.4 us
    pallas_call x1, Pallas kernels, place(): pl.pallas_call(place_kernel, grid_spec=pltpu.PrefetchScalarGridSpec(num_s...  41 us
  transfers between devices with their start and end apart: 18, of which 8 were waited for; matrix products, arithmetic and copies ran while one was open for 6% of the time, Pallas kernels for 8%

profile of v2, /device:TPU:24, one launch (start us, length us, event | category | flops | bytes accessed | tf_op | source)
XLA Modules:
  0.0 1169.4 jit_solution(2804776319274681831)
XLA Ops:
  8.0 0.7 all-gather.4.cloned.1.call-update
  8.8 3.3 abs_reduce_fusion
  12.1 0.1 slice.48
  12.2 0.2 slice.47
  12.5 2.0 pad_maximum_fusion
  14.5 51.5 %pmax.7 = f32[]{:T(128)} all-reduce(f32[]{:T(128)} %get-tuple-element.23), channel_id=1, replica_groups=mesh['child'=2,'row'=4,'col'=4] {'child','row','col'}, use_global_device_ids=true, to_apply=%region_3.4 | all-reduce | flops 1 | bytes 8 | tf_op jit(solution)/shard_map/pmax | solution.py:247
  66.7 0.1 select_reduce_fusion
  66.8 252.8 %all-gather.4.cloned.1.call-done.full_ref = f32[4,1024,1024]{2,1,0:T(8,128)} async-done(((f32[1,1024,1024]{2,1,0:T(8,128)}), f32[4,1024,1024]{2,1,0:T(8,128)}) %all-gather.4.cloned.1.call-update) | async-done | bytes 16777232 | tf_op jit(solution)/shard_map/all_gather | solution.py:245
  319.6 41.0 %shard_map.58 = f32[8,1024,1024]{2,1,0:T(8,128)} custom-call(s32[64]{0:T(128)S(1)} %fusion.22.src_ref, f32[4,1024,1024]{2,1,0:T(8,128)} %all-gather.4.cloned.1.call-done.full_ref), custom_call_target="tpu_custom_call" | custom-call | bytes 50331648 | tf_op jit(solution)/shard_map/pallas_call | solution.py:106
  360.6 18.9 %multiply_convert_fusion = f16[8,1024,1024]{2,1,0:T(8,128)(2,1)} fusion(f32[8,1024,1024]{2,1,0:T(8,128)} %shard_map.58, f32[]{:T(128)S(6)} %div.4), kind=kLoop, calls=%fused_computation.1 | loop fusion | flops 16777216 | bytes 50331652 | tf_op jit(solution)/shard_map/convert_element_type | solution.py:249
  379.4 42.7 %all-reduce.4.cloned.1.call-done = f32[1536,512]{1,0:T(8,128)} async-done(((f32[1536,512]{1,0:T(8,128)}), f32[1536,512]{1,0:T(8,128)}) %all-reduce.4.cloned.1.call-update) | async-done | bytes 3145744 | tf_op jit(solution)/shard_map/psum | solution.py:244
  422.2 1.4 slice.39.a_ref
  423.6 54.1 %shard_map.59 = f32[512,512]{1,0:T(8,128)S(1)} custom-call(f32[512,512]{1,0:T(8,128)S(1)} %slice.39.a_ref), custom_call_target="tpu_custom_call" | custom-call | flops 1000000 | bytes 2097152 | tf_op jit(solution)/shard_map/pallas_call | solution.py:75
  477.7 1.9 convolution_convert_fusion
  479.6 0.5 convolution_subtract_fusion.1.a_ref
  480.1 54.4 %shard_map.60 = f32[512,512]{1,0:T(8,128)S(1)} custom-call(f32[512,512]{1,0:T(8,128)S(1)} %convolution_subtract_fusion.1.a_ref), custom_call_target="tpu_custom_call" | custom-call | flops 1000000 | bytes 2097152 | tf_op jit(solution)/shard_map/pallas_call | solution.py:75
  534.5 2.5 slice_bitcast_fusion
  537.0 4.9 select_convert_fusion.4
  541.9 0.8 fusion.25
  542.7 3.6 select_convert_fusion.3
  546.3 1.5 pad_maximum_fusion.1
  547.8 5.7 all-to-all-start
  553.7 250.6 %all-to-all-done = f16[8,1024,1024]{2,1,0:T(8,128)(2,1)} async-done(((f16[8,1024,1024]{2,1,0:T(8,128)(2,1)}), f16[8,1024,1024]{2,1,0:T(8,128)(2,1)}, u32[]{:S(2)}, u32[]{:S(2)}) %all-to-all-start) | async-done | bytes 16777248 | tf_op jit(solution)/shard_map/all_to_all | solution.py:256
  804.4 18.8 %convert_multiply_fusion.got0.got1 = f32[8,1024,1024]{2,1,0:T(8,128)} fusion(f16[8,1024,1024]{2,1,0:T(8,128)(2,1)} %all-to-all-done, f32[]{:T(128)S(6)} %mul.38), kind=kLoop, calls=%fused_computation | loop fusion | flops 16777216 | bytes 50331652 | tf_op jit(solution)/shard_map/mul | solution.py:257
  823.1 22.4 %copy.10 = bf16[8192,1024]{1,0:T(8,128)(2,1)} copy(bf16[8192,1024]{0,1:T(8,128)(2,1)} %all-gather.6.cloned.1.call-done) | data formatting | bytes 33554432 | tf_op jit(solution)/shard_map/all_gather | solution.py:267
  845.5 6.2 shard_map.61.cols_ref
  851.8 22.1 %shard_map.62 = f32[2048,1024]{1,0:T(8,128)} custom-call(s32[2,16]{1,0:T(2,128)S(1)} %constant_dynamic-slice_fusion.1.src_ref, f32[2048,1024]{1,0:T(8,128)} %root_ref.1, f32[8,1024,1024]{2,1,0:T(8,128)} %convert_multiply_fusion.got0.got1, f32[8,1024,1024]{2,1,0:T(8,128)} %convert_multiply_fusion.got0.got1, bf16[8,1024,1024]{2,1,0:T(8,128)(2,1)} %bitcast.23, ...), custom_call_target="tpu_custom_call" | custom-call | tf_op jit(solution)/shard_map/pallas_call | solution.py:177
  873.8 1.1 split.16
  874.9 0.7 collective-permute-start
  875.7 2.8 broadcast_select_fusion.3
  878.4 0.7 collective-permute-start.3
  879.1 1.5 collective-permute-start.6
  880.6 1.6 collective-permute-start.9
  882.2 4.6 slice_select_fusion
  886.8 2.3 slice_select_fusion.1
  889.2 1.5 collective-permute-start.1
  890.7 0.8 copy-done.4
  891.5 2.7 broadcast_select_fusion.2
  894.2 1.4 collective-permute-start.10
  895.6 4.1 maximum_bitcast_fusion
  899.8 5.3 copy.11
  905.1 131.0 %all-reduce.8.cloned.1.call-done.a_ref = f32[512,512]{1,0:T(8,128)} async-done(((f32[512,512]{1,0:T(8,128)}), f32[512,512]{1,0:T(8,128)}) %all-reduce.8.cloned.1.call-update) | async-done | bytes 1048592 | tf_op jit(solution)/shard_map/psum | solution.py:278
  1036.1 1.2 copy-done
  1037.4 54.1 %shard_map.63 = f32[512,512]{1,0:T(8,128)S(1)} custom-call(f32[512,512]{1,0:T(8,128)S(1)} %copy-done), custom_call_target="tpu_custom_call" | custom-call | flops 1000000 | bytes 2097152 | tf_op jit(solution)/shard_map/pallas_call | solution.py:75
  1091.5 0.7 collective-permute-start.7
  1092.2 0.7 collective-permute-start.4
  1092.9 0.1 broadcast_select_fusion.7
  1093.0 1.3 collective-permute-start.2
  1094.3 1.1 broadcast_select_fusion.4
  1095.4 1.3 collective-permute-start.11
  1096.7 0.1 broadcast_select_fusion.5
  1096.8 1.3 collective-permute-start.8
  1098.1 0.1 broadcast_select_fusion.6
  1098.2 1.5 collective-permute-start.5
  1099.7 10.3 collective-permute-done.2
  1110.0 0.1 broadcast_select_fusion.11
  1110.0 11.2 collective-permute-done.11
  1121.2 0.1 broadcast_select_fusion.8
  1121.3 11.2 collective-permute-done.8
  1132.5 8.9 collective-permute-done.5
  1141.3 0.1 broadcast_select_fusion.10
  1141.4 3.6 select_convert_fusion.2
  1145.0 8.6 fusion.26
  1153.6 8.4 convolution_subtract_fusion
  (36 shorter events, 0.6 us)
Async XLA Ops:
  8.0 311.6 %all-gather.4.cloned.1.call-start = ((), (), s32[]{:S(2)}) async-start(), calls=%async_computation.2 | async-start | bytes 20971520 | tf_op jit(solution)/shard_map/all_gather | solution.py:245
  8.7 413.4 %all-reduce.4.cloned.1.call-start = ((), (), s32[]{:S(2)}) async-start(), calls=%async_computation.1 | async-start | bytes 6291456 | tf_op jit(solution)/shard_map/psum | solution.py:244
  12.4 54.3 %copy-start.5 = (s32[2,24]{1,0:T(2,128)S(1)}, s32[2,24]{1,0:T(2,128)}, u32[]{:S(2)}) copy-start(s32[2,24]{1,0:T(2,128)} %param.5) | copy-start | bytes 580
  14.5 808.7 %all-gather.6.cloned.1.call-start = ((), (), s32[]{:S(2)}) async-start(), calls=%async_computation.5 | async-start | bytes 18874368 | tf_op jit(solution)/shard_map/all_gather | solution.py:267
  422.2 55.6 %copy-start.2 = (f32[1536,512]{1,0:T(8,128)S(1)}, f32[1536,512]{1,0:T(8,128)}, u32[]{:S(2)}) copy-start(f32[1536,512]{1,0:T(8,128)} %all-reduce.4.cloned.1.call-done) | copy-start | bytes 9437188
  547.8 256.5 %all-to-all-start = ((f16[8,1024,1024]{2,1,0:T(8,128)(2,1)}), f16[8,1024,1024]{2,1,0:T(8,128)(2,1)}, u32[]{:S(2)}, u32[]{:S(2)}) async-start(f16[8,1024,1024]{2,1,0:T(8,128)(2,1)} %multiply_convert_fusion), calls=%async_computation | async-start | bytes 33554432 | tf_op jit(solution)/shard_map/all_to_all | solution.py:256
  553.5 482.6 %all-reduce.8.cloned.1.call-start = ((), (), s32[]{:S(2)}) async-start(), calls=%async_computation.4 | async-start | bytes 2097152 | tf_op jit(solution)/shard_map/psum | solution.py:278
  874.9 0.7 collective-permute-start
  878.4 12.2 %collective-permute-start.3 = (f32[128,1024]{1,0:T(8,128)}, f32[128,1024]{1,0:T(8,128)S(1)}, u32[]{:S(2)}, u32[]{:S(2)}) collective-permute-start(f32[128,1024]{1,0:T(8,128)} %get-tuple-element.19), channel_id=1, source_target_pairs={{0,1},{4,5},{8,9},{12,13},{16,17},{20,21},{24,25},{28,29}} | collective-permute-start | bytes 1572872 | tf_op jit(solution)/shard_map/ppermute | solution.py:209
  879.1 11.5 collective-permute-start.6
  880.6 10.9 collective-permute-start.9
  889.1 255.9 %all-reduce.6.cloned.1.call-start = ((), (), s32[]{:S(2)}) async-start(), calls=%async_computation.3 | async-start | bytes 8388608 | tf_op jit(solution)/shard_map/psum | solution.py:280
  889.2 203.7 %collective-permute-start.1 = (f32[128,1024]{1,0:T(8,128)S(1)}, f32[128,1024]{1,0:T(8,128)}, u32[]{:S(2)}, u32[]{:S(2)}) collective-permute-start(f32[128,1024]{1,0:T(8,128)S(1)} %get-tuple-element.16), channel_id=1, source_target_pairs={{1,2},{5,6},{9,10},{13,14},{17,18},{21,22},{25,26},{29,30}} | collective-permute-start | bytes 1572872 | tf_op jit(solution)/shard_map/ppermute | solution.py:209
  890.7 0.8 copy-start.4
  894.2 200.1 %collective-permute-start.10 = (f32[128,1024]{1,0:T(8,128)}, f32[128,1024]{1,0:T(8,128)}, u32[]{:S(2)}, u32[]{:S(2)}) collective-permute-start(f32[128,1024]{1,0:T(8,128)} %get-tuple-element.22), channel_id=1, source_target_pairs={{1,2},{5,6},{9,10},{13,14},{17,18},{21,22},{25,26},{29,30}} | collective-permute-start | bytes 1572872 | tf_op jit(solution)/shard_map/ppermute | solution.py:209
  905.1 186.4 %copy-start.3 = (f32[128,1024]{1,0:T(8,128)S(1)}, f32[128,1024]{1,0:T(8,128)}, u32[]{:S(2)}) copy-start(f32[128,1024]{1,0:T(8,128)} %get-tuple-element.21) | copy-start | bytes 1572868
  1036.1 1.2 copy-start
  1091.5 5.2 collective-permute-start.7
  1092.2 5.9 collective-permute-start.4
  1093.0 17.0 %collective-permute-start.2 = (f32[128,1024]{1,0:T(8,128)S(1)}, f32[128,1024]{1,0:T(8,128)S(1)}, u32[]{:S(2)}, u32[]{:S(2)}) collective-permute-start(f32[128,1024]{1,0:T(8,128)S(1)} %broadcast_select_fusion.7), channel_id=1, source_target_pairs={{2,3},{6,7},{10,11},{14,15},{18,19},{22,23},{26,27},{30,31}} | collective-permute-start | bytes 1572872 | tf_op jit(solution)/shard_map/ppermute | solution.py:209
  1095.4 25.8 %collective-permute-start.11 = (f32[128,1024]{1,0:T(8,128)S(1)}, f32[128,1024]{1,0:T(8,128)S(1)}, u32[]{:S(2)}, u32[]{:S(2)}) collective-permute-start(f32[128,1024]{1,0:T(8,128)S(1)} %broadcast_select_fusion.4), channel_id=1, source_target_pairs={{2,3},{6,7},{10,11},{14,15},{18,19},{22,23},{26,27},{30,31}} | collective-permute-start | bytes 1572872 | tf_op jit(solution)/shard_map/ppermute | solution.py:209
  1096.8 35.6 %collective-permute-start.8 = (f32[128,1024]{1,0:T(8,128)S(1)}, f32[128,1024]{1,0:T(8,128)S(1)}, u32[]{:S(2)}, u32[]{:S(2)}) collective-permute-start(f32[128,1024]{1,0:T(8,128)S(1)} %broadcast_select_fusion.5), channel_id=1, source_target_pairs={{2,3},{6,7},{10,11},{14,15},{18,19},{22,23},{26,27},{30,31}} | collective-permute-start | bytes 1572872 | tf_op jit(solution)/shard_map/ppermute | solution.py:209
  1098.2 43.2 %collective-permute-start.5 = (f32[128,1024]{1,0:T(8,128)S(1)}, f32[128,1024]{1,0:T(8,128)S(1)}, u32[]{:S(2)}, u32[]{:S(2)}) collective-permute-start(f32[128,1024]{1,0:T(8,128)S(1)} %broadcast_select_fusion.6), channel_id=1, source_target_pairs={{2,3},{6,7},{10,11},{14,15},{18,19},{22,23},{26,27},{30,31}} | collective-permute-start | bytes 1572872 | tf_op jit(solution)/shard_map/ppermute | solution.py:209
  1153.6 8.4 copy-start.1
Sparse Core Ops, SparseCore 0:
  10.5 309.0 all-gather.3
  889.2 146.8 all-reduce.7
  1039.4 81.1 all-reduce.5
Sparse Core Ops, SparseCore 1:
  15.4 406.7 all-reduce.3
  547.9 244.8 all-gather.5
